TPU v7x, 32 devices: a whole 2x2x4 slice. The times are simulated.
32 devices in a mesh: row: 4 (over z), col: 8 (over y, x, core).
Axes of the slice: x: 2, y: 2, z: 4, core: 2. Of those that a mesh axis runs over, the one named last changes fastest.
Arguments:
- valence: bfloat16 [32, 2, 64000], P(('row', 'col')), may hold values from -2.09375 to 2.09375
- conduction: bfloat16 [128, 2, 64000], P(('row', 'col')), may hold values from -2.09375 to 2.09375
- valence_slot_index: int32 [2], replicated, may hold values from 0 to 31
- weights: float32 [2, 128], P(None, ('row', 'col')), may hold values from 0.1 to 1
- sphere_index: int32 [9984], replicated, may hold values from 0 to 63999, as said below
Outputs:
- polarizability: float32 [2, 9984, 9984], P(None, 'row', 'col')
Inputs may be any that keep to these rules, and one draw needn't show every extreme that they name: `sphere_index`: all entries are distinct.
All inputs are finite; a program needn't handle non-finite values.
Results may differ from a plain program's by a relative error of at most 0.0039.
Values may be sent and summed in bfloat16 or wider, within the bound.
A program may use at most 256 MiB of HBM per device.

v0:
```python
import math

import jax
import jax.numpy as jnp
from jax import lax
from jax.sharding import PartitionSpec as P

NBOX = 40


def broadcast(block, axis, owner):
    block = jnp.where(lax.axis_index(axis) == owner, block, jnp.zeros_like(block))
    return lax.psum(block, axis)


def plane_table(count):
    square = count * count
    ident = jnp.arange(square, dtype=jnp.int32)
    first_idx = ident // count
    second_idx = ident % count
    phase_steps = (
        first_idx[:, None] * first_idx[None, :] + second_idx[:, None] * second_idx[None, :]
    ) % count
    angle_plane = 2.0 * math.pi / count * phase_steps.astype(jnp.float32)
    cosine_plane = jnp.cos(angle_plane) / count
    sine_plane = jnp.sin(angle_plane) / count
    upper = jnp.concatenate([cosine_plane, -sine_plane], axis=1)
    lower = jnp.concatenate([sine_plane, cosine_plane], axis=1)
    return jnp.concatenate([upper, lower], axis=0)


def axis_table(count):
    ident = jnp.arange(count, dtype=jnp.int32)
    phase_steps = ident[:, None] * ident[None, :] % count
    angle_line = 2.0 * math.pi / count * phase_steps.astype(jnp.float32)
    cosine_line = jnp.cos(angle_line) / math.sqrt(count)
    sine_line = jnp.sin(angle_line) / math.sqrt(count)
    real_row = jnp.stack([cosine_line, sine_line], axis=-1)
    imag_row = jnp.stack([-sine_line, cosine_line], axis=-1)
    return jnp.stack([real_row, imag_row], axis=1)


def transform_pick(dens_re, dens_im, count, sphere_index):
    pairs = dens_re.shape[0]
    square = count * count
    high = lax.Precision.HIGHEST
    joined = jnp.stack(
        [dens_re.reshape(pairs, count, square), dens_im.reshape(pairs, count, square)], axis=2
    )
    planes = jnp.dot(joined.reshape(pairs * count, 2 * square), plane_table(count), precision=high)
    planes = planes.reshape(pairs, count, 2, square)
    spectrum = jnp.einsum("kfad,pady->kfpy", axis_table(count), planes, precision=high)
    first_freq = sphere_index // square
    plane_freq = sphere_index % square
    picked = spectrum[first_freq, :, :, plane_freq]
    return jnp.transpose(picked, (2, 1, 0))


def on_device(valence, conduction, valence_slot_index, weights, sphere_index):
    rows = lax.axis_size("row")
    cols = lax.axis_size("col")
    nbands = weights.shape[0]
    stored = valence[0]
    bands = jnp.stack(
        [broadcast(stored, ("row", "col"), valence_slot_index[band]) for band in range(nbands)]
    )
    chosen = bands.astype(jnp.float32)
    states = conduction.astype(jnp.float32)
    val_re = chosen[:, 0][:, None, :]
    val_im = chosen[:, 1][:, None, :]
    con_re = states[:, 0][None, :, :]
    con_im = states[:, 1][None, :, :]
    device_pairs = nbands * conduction.shape[0]
    dens_re = (val_re * con_re + val_im * con_im).reshape(device_pairs, -1)
    dens_im = (val_re * con_im - val_im * con_re).reshape(device_pairs, -1)
    values = transform_pick(dens_re, dens_im, NBOX, sphere_index)
    plain = values.astype(jnp.bfloat16)
    scaled = (weights.reshape(device_pairs)[:, None, None] * values).astype(jnp.bfloat16)
    regrouped = lax.all_to_all(scaled, "row", split_axis=2, concat_axis=0, tiled=True)
    row_block = lax.all_gather(regrouped, "col", axis=0, tiled=True)
    left = row_block.reshape(cols, rows, device_pairs, 2, row_block.shape[-1])
    spread = lax.all_to_all(plain, "col", split_axis=2, concat_axis=0, tiled=True)
    moved = lax.all_gather(spread, "row", axis=0, tiled=True)
    right = moved.reshape(rows, cols, device_pairs, 2, moved.shape[-1])
    order = "ijp"
    real_part = jnp.einsum(
        "jipcr," + order + "cs->rs", left, right, preferred_element_type=jnp.float32
    )
    imag_one = jnp.einsum(
        "jipr," + order + "s->rs",
        left[:, :, :, 1],
        right[:, :, :, 0],
        preferred_element_type=jnp.float32,
    )
    imag_two = jnp.einsum(
        "jipr," + order + "s->rs",
        left[:, :, :, 0],
        right[:, :, :, 1],
        preferred_element_type=jnp.float32,
    )
    return jnp.stack([real_part, imag_one - imag_two])


def solution(mesh):
    placed = (
        P(("row", "col"), None, None),
        P(("row", "col"), None, None),
        P(),
        P(None, ("row", "col")),
        P(),
    )
    return jax.shard_map(
        on_device, mesh=mesh, in_specs=placed, out_specs=P(None, "row", "col"), check_vma=False
    )
```

profile of v0, /device:TPU:0, one launch (start us, length us, event | category | flops | bytes accessed | tf_op | source)
XLA Modules:
  0.0 545.1 jit_solution(13492193454215043823)
XLA Ops:
  6.5 0.0 all-reduce.3.cloned.1.call-start
  6.5 1.3 fusion.41
  9.1 2.1 broadcast_select_fusion.1
  11.3 0.0 all-reduce.3.cloned.1.call-update
  11.3 0.0 all-gather.5.cloned.1.call-start
  11.4 3.3 fusion.40
  14.7 0.0 copy-done
  14.7 0.1 fusion.20
  14.7 47.7 %fusion.15 = (f32[1600,1600]{0,1:T(8,128)S(1)}, f32[1600,1600]{0,1:T(8,128)}, f32[1600,1600]{0,1:T(8,128)}) fusion(s32[1600]{0:T(1024)S(1)} %get-tuple-element.24, s32[1600]{0:T(1024)S(1)} %get-tuple-element.25), kind=kLoop, calls=%fused_computation.26 | loop fusion | flops 35840000 | bytes 30732800 | tf_op jit(solution)/shard_map/neg | solution.py:27
  62.4 0.5 copy_bitcast_fusion
  62.9 0.0 copy-start.3
  63.0 35.2 %maximum_maximum_fusion = f32[3200,3200]{0,1:T(8,128)} fusion(f32[1600,1600]{0,1:T(8,128)} %get-tuple-element.21, f32[1600,1600]{0,1:T(8,128)} %get-tuple-element.20, f32[1600,1600]{0,1:T(8,128)S(1)} %get-tuple-element.19), kind=kLoop, calls=%fused_computation.1 | loop fusion | flops 30720000 | bytes 71680000 | tf_op jit(solution)/shard_map/concatenate | solution.py:29
  98.1 0.1 fusion.33
  98.2 0.0 copy-done.3
  98.2 0.1 mul.246
  98.3 0.1 sine_multiply_fusion.1
  98.4 45.2 %all-reduce.3.cloned.1.call-done = (bf16[1,2,64000]{2,1,0:T(2,128)(2,1)}, bf16[1,2,64000]{2,1,0:T(2,128)(2,1)}) async-done(((bf16[1,2,64000]{2,1,0:T(2,128)(2,1)}, bf16[1,2,64000]{2,1,0:T(2,128)(2,1)}), (bf16[1,2,64000]{2,1,0:T(2,128)(2,1)}, bf16[1,2,64000]{2,1,0:T(2,128)(2,1)})) %all-reduce.3.cloned.1.call-update) | async-done | bytes 512016 | tf_op jit(solution)/shard_map/psum | solution.py:13
  143.6 1.7 maximum_convert_fusion
  145.3 0.8 fusion.39
  146.1 0.5 copy_bitcast_fusion.2
  146.7 2.5 multiply_add_fusion
  149.2 4.7 sub.35
  153.9 6.0 %add.118 = f32[8,40,1,1600]{3,2,1,0:T(1,128)} reshape(f32[2,4,64000]{2,1,0:T(4,128)} %get-tuple-element.9) | data formatting | bytes 4096000 | tf_op jit(solution)/shard_map/add | solution.py:74
  159.9 7.5 %pad_maximum_fusion.1 = f32[8,40,2,1600]{3,2,1,0:T(2,128)} fusion(f32[8,40,1,1600]{3,2,1,0:T(1,128)S(1)} %sub.35, f32[8,40,1,1600]{3,2,1,0:T(1,128)} %add.118), kind=kLoop, calls=%fused_computation.20 | loop fusion | flops 1024000 | bytes 8192000 | tf_op jit(solution)/shard_map/stack | solution.py:47
  167.4 5.9 %reshape.229 = f32[8,40,3200,1]{2,1,0,3:T(8,128)} reshape(f32[8,40,2,1600]{3,2,1,0:T(2,128)} %pad_maximum_fusion.1) | data formatting | bytes 8192000 | tf_op jit(solution)/shard_map/dot_general | solution.py:50
  173.3 55.9 %fusion.10 = f32[8,40,2,1600]{3,1,2,0:T(8,128)S(1)} fusion(f32[2,1600,3200,1]{2,1,0,3:T(8,128)} %bitcast.88, f32[8,40,3200,1]{2,1,0,3:T(8,128)} %reshape.229), kind=kOutput, calls=%fused_computation.23 | convolution fusion | flops 39321600000 | bytes 49152000 | tf_op jit(solution)/shard_map/dot_general | solution.py:50
  229.3 5.7 %fusion.12 = f32[40,2,8,1600]{3,0,2,1:T(8,128)} fusion(f32[8,40,2,1600]{3,1,2,0:T(8,128)S(1)} %fusion.10, f32[40,1,40,2]{2,0,3,1:T(8,128)S(1)} %get-tuple-element.18, f32[40,1,40,2]{2,0,3,1:T(8,128)S(1)} %get-tuple-element.17), kind=kOutput, calls=%fused_computation.25 | convolution fusion | flops 983046400 | bytes 8217600 | tf_op jit(solution)/shard_map/kfad,pady->kfpy/dot_general | solution.py:52
  234.9 49.3 %copy.12 = f32[40,2,8,1600]{2,1,3,0:T(2,128)} copy(f32[40,2,8,1600]{3,0,2,1:T(8,128)} %fusion.12) | data formatting | bytes 8192000 | tf_op jit(solution)/shard_map/kfad,pady->kfpy/dot_general | solution.py:52
  284.2 103.5 %gather_fusion = f32[9984,2,8]{2,1,0:T(2,128)} fusion(f32[40,2,8,1600]{2,1,3,0:T(2,128)} %copy.12, s32[9984]{0:T(1024)S(1)} %fusion.20), kind=kCustom, calls=%fused_computation | custom fusion | bytes 1357824 | tf_op jit(solution)/shard_map/gather | solution.py:55
  387.6 12.7 %convert_bitcast_fusion = (bf16[8,2,9984]{0,1,2:T(2,128)(2,1)}, bf16[8,2,9984]{0,1,2:T(2,128)(2,1)}) fusion(f32[9984,2,8]{2,1,0:T(2,128)} %gather_fusion, f32[8]{0:T(128)S(1)} %mul.246), kind=kLoop, calls=%fused_computation.19 | loop fusion | flops 479232 | bytes 1277984 | tf_op jit(solution)/shard_map/convert_element_type | solution.py:77
  400.3 6.7 %reshape.240 = bf16[8,2,9984]{2,1,0:T(2,128)(2,1)S(1)} reshape(bf16[9984,2,8]{2,1,0:T(2,128)(2,1)} %bitcast.90) | data formatting | bytes 638976
  407.1 10.9 %all_to_all.36 = bf16[8,2,9984]{2,1,0:T(2,128)(2,1)S(1)} all-to-all(bf16[8,2,9984]{2,1,0:T(2,128)(2,1)S(1)} %reshape.240), channel_id=1, replica_groups=mesh['row'=4,'col'=8] {'col'}, dimensions={0} | all-to-all | bytes 638976 | tf_op jit(solution)/shard_map/all_to_all | solution.py:82
  418.0 7.0 %reshape.241 = bf16[9984,2,8]{2,1,0:T(2,128)(2,1)} reshape(bf16[8,2,9984]{2,1,0:T(2,128)(2,1)S(1)} %all_to_all.36) | data formatting | bytes 638976
  425.1 10.5 %copy.26 = bf16[8,2,8,1248]{3,0,2,1:T(8,128)(2,1)} copy(bf16[8,2,8,1248]{0,1,3,2:T(2,128)(2,1)} %bitcast.91) | data formatting | bytes 638976 | tf_op jit(solution)/shard_map/all_to_all | solution.py:82
  435.6 0.0 all-gather.5.cloned.1.call-update
  435.6 0.0 all-gather.3.cloned.1.call-start
  435.7 6.7 %reshape.238 = bf16[4,2,19968]{2,1,0:T(2,128)(2,1)S(1)} reshape(bf16[9984,2,8]{2,1,0:T(2,128)(2,1)} %bitcast.89) | data formatting | bytes 638976
  442.4 22.0 %all_to_all.37 = bf16[4,2,19968]{2,1,0:T(2,128)(2,1)S(1)} all-to-all(bf16[4,2,19968]{2,1,0:T(2,128)(2,1)S(1)} %reshape.238), channel_id=1, replica_groups=mesh['row'=4,'col'=8] {'row'}, dimensions={0} | all-to-all | bytes 638976 | tf_op jit(solution)/shard_map/all_to_all | solution.py:79
  464.4 7.0 %reshape.239 = bf16[9984,2,8]{2,1,0:T(2,128)(2,1)} reshape(bf16[4,2,19968]{2,1,0:T(2,128)(2,1)S(1)} %all_to_all.37) | data formatting | bytes 638976
  471.5 10.5 %copy.13 = bf16[8,2,4,2496]{3,0,2,1:T(8,128)(2,1)} copy(bf16[8,2,4,2496]{0,1,3,2:T(2,128)(2,1)} %bitcast.92) | data formatting | bytes 638976 | tf_op jit(solution)/shard_map/all_to_all | solution.py:79
  482.0 0.0 all-gather.3.cloned.1.call-update
  482.0 0.0 all-gather.5.cloned.1.call-done
  482.0 28.4 %all-gather.3.cloned.1.call-done = bf16[256,2,2496]{2,0,1:T(8,128)(2,1)} async-done(((bf16[32,2,2496]{2,0,1:T(8,128)(2,1)}), bf16[256,2,2496]{2,0,1:T(8,128)(2,1)}) %all-gather.3.cloned.1.call-update) | async-done | bytes 2555920 | tf_op jit(solution)/shard_map/all_gather | solution.py:80
  510.4 8.3 %convolution_bitcast_fusion.1 = f32[2496,1248]{1,0:T(8,128)} fusion(bf16[4,8,8,2,1248]{4,2,1,0,3:T(8,128)(2,1)} %bitcast.98, bf16[8,4,8,2,2496]{4,2,1,0,3:T(8,128)(2,1)} %bitcast.95), kind=kOutput, calls=%fused_computation.7 | convolution fusion | flops 1594884096 | bytes 14426112 | tf_op jit(solution)/shard_map/jipr,ijps->rs/dot_general | solution.py:89
  518.8 0.0 copy-done.2
  518.8 3.5 convolution_bitcast_fusion.2
  522.3 7.1 %fusion.1 = f32[1,2496,1248]{2,1,0:T(8,128)S(1)} fusion(f32[2496,1248]{1,0:T(8,128)} %convolution_bitcast_fusion.1, bf16[4,8,8,2,1248]{4,2,1,0,3:T(8,128)(2,1)} %bitcast.99, bf16[8,4,8,2,2496]{4,2,1,0,3:T(8,128)(2,1)} %bitcast.96), kind=kOutput, calls=%fused_computation.6 | convolution fusion | flops 1597999104 | bytes 27205632 | tf_op jit(solution)/shard_map/jipr,ijps->rs/dot_general | solution.py:95
  529.4 8.9 %pad_maximum_fusion = f32[2,2496,1248]{2,1,0:T(8,128)} fusion(f32[1,2496,1248]{2,1,0:T(8,128)S(1)} %fusion.1, f32[1,2496,1248]{2,1,0:T(8,128)S(1)} %convolution_bitcast_fusion.2), kind=kLoop, calls=%fused_computation.2 | loop fusion | flops 6230016 | bytes 49840128 | tf_op jit(solution)/shard_map/stack | solution.py:101
  (6 shorter events, 0.0 us)
Async XLA Ops:
  6.5 8.1 %copy-start = (s32[9984]{0:T(1024)S(1)}, s32[9984]{0:T(1024)}, u32[]{:S(2)}) copy-start(s32[9984]{0:T(1024)} %param.9) | copy-start | bytes 119812
  6.5 137.1 %all-reduce.3.cloned.1.call-start = ((), (), s32[]{:S(2)}) async-start(), calls=%async_computation.4 | async-start | bytes 1024000 | tf_op jit(solution)/shard_map/psum | solution.py:13
  11.3 470.7 %all-gather.5.cloned.1.call-start = ((), (), s32[]{:S(2)}) async-start(), calls=%async_computation.3 | async-start | bytes 1638400 | tf_op jit(solution)/shard_map/all_gather | solution.py:83
  62.9 35.3 %copy-start.3 = (f32[2,4]{1,0:T(2,128)S(1)}, f32[2,4]{1,0:T(2,128)}, u32[]{:S(2)}) copy-start(f32[2,4]{1,0:T(2,128)} %param.8) | copy-start | bytes 100
  435.6 74.8 %all-gather.3.cloned.1.call-start = ((), (), s32[]{:S(2)}) async-start(), calls=%async_computation.2 | async-start | bytes 2949120 | tf_op jit(solution)/shard_map/all_gather | solution.py:80
  510.4 8.3 %copy-start.1 = (bf16[256,2,2496]{2,0,1:T(8,128)(2,1)S(1)}, bf16[256,2,2496]{2,0,1:T(8,128)(2,1)}, u32[]{:S(2)}) copy-start(bf16[256,2,2496]{2,0,1:T(8,128)(2,1)} %all-gather.3.cloned.1.call-done) | copy-start | bytes 7667716
  510.4 8.3 %copy-start.2 = (bf16[256,2,1248]{2,0,1:T(8,128)(2,1)S(1)}, bf16[256,2,1248]{2,0,1:T(8,128)(2,1)}, u32[]{:S(2)}) copy-start(bf16[256,2,1248]{2,0,1:T(8,128)(2,1)} %all-gather.5.cloned.1.call-done) | copy-start | bytes 3833860
Sparse Core Ops, SparseCore 0:
  12.7 130.8 all-reduce.2
  435.7 37.0 all-gather.4
  482.1 28.2 all-gather.2
where the time goes:
time: 553 us; the launch traced here: 545 us
  local copies, waits for them, and re-layouts  224 us (41%)
  other arithmetic  119 us (22%)
  matrix products  80.6 us (15%)
  waiting for transfers between devices  73.6 us (13%)
  blocking collectives  33 us (6%)
  between operations  14.8 us (3%)
    gather x1, local copies, waits for them, and re-layouts, transform_pick(): picked = spectrum[first_freq, :, :, plane_freq]  103 us
    dot_general x1, matrix products, transform_pick(): jnp.dot(joined.reshape(pairs * count, 2 * square), plane_table(count), pr...  55.9 us
    dot_general x1, local copies, waits for them, and re-layouts, transform_pick(): jnp.einsum('kfad,pady->kfpy', axis_table(count), planes, precision=high)  49.3 us
    neg x1, other arithmetic, plane_table(): upper = jnp.concatenate([cosine_plane, -sine_plane], axis=1)  47.7 us
    psum x1, waiting for transfers between devices, broadcast(): return lax.psum(block, axis)  45.2 us
    concatenate x1, other arithmetic, plane_table(): return jnp.concatenate([upper, lower], axis=0)  35.2 us
    unnamed x14, local copies, waits for them, and re-layouts  28.6 us
    all_gather x1, waiting for transfers between devices, on_device(): row_block = lax.all_gather(regrouped, 'col', axis=0, tiled=True)  28.4 us
  transfers between devices with their start and end apart: 3, of which 2 were waited for; matrix products, arithmetic and copies ran while one was open for 20% of the time, Pallas kernels for 0%

commit v1 on v0

v1 whole, which is shorter than its diff:
```python
import functools
import math

import jax
import jax.numpy as jnp
import ml_dtypes
import numpy as np
from jax import lax
from jax.experimental import pallas as pl
from jax.experimental.pallas import tpu as pltpu
from jax.sharding import PartitionSpec as P

NBOX = 40
RADIX = 4
VMEM = 56 * 1024 * 1024
BF = jnp.bfloat16
F32 = jnp.float32


def split_host(table):
    high = table.astype(np.float32).astype(ml_dtypes.bfloat16)
    low = (table - high.astype(np.float64)).astype(ml_dtypes.bfloat16)
    return np.stack([high, low])


def host_tables(count, pairs):
    square = count * count
    part = square // RADIX
    wide = -(-part // 128) * 128
    rows = np.arange(part)
    tables = []
    for residue in range(RADIX):
        freq_b = RADIX * (rows // count) + residue
        freq_e = rows % count
        steps = (np.outer(rows // count, freq_b) + np.outer(rows % count, freq_e)) % count
        angle = 2.0 * math.pi / count * steps
        both = np.zeros((2, part, wide))
        both[0, :, :part] = np.cos(angle) / count
        both[1, :, :part] = np.sin(angle) / count
        tables.append(split_host(both))
    plane = np.stack(tables)
    line = np.arange(count)
    angle = 2.0 * math.pi / count * (np.outer(line, line) % count)
    cosine, sine = np.cos(angle) / math.sqrt(count), np.sin(angle) / math.sqrt(count)
    first = np.zeros((count, 2, pairs, 2, pairs, count))
    for pair in range(pairs):
        first[:, 0, pair, 0, pair] = cosine
        first[:, 0, pair, 1, pair] = sine
        first[:, 1, pair, 0, pair] = -sine
        first[:, 1, pair, 1, pair] = cosine
    size = 2 * pairs * count
    return plane, split_host(first.reshape(size, size)), part, wide


def dft_kernel(nbands, count, val_ref, con_ref, plane_ref, first_ref, out_ref, x_ref):
    step = pl.program_id(0)
    half = x_ref.shape[1] // 2
    block = con_ref.shape[2]
    bands = block // count

    @pl.when(step == 0)
    def _():
        for band in range(nbands):
            re, im = [], []
            for quarter in range(RADIX):
                con_re = con_ref[0, quarter].astype(F32)
                con_im = con_ref[1, quarter].astype(F32)
                own = slice(band * count, (band + 1) * count)
                val_re = val_ref[0, quarter].astype(F32)[own]
                val_im = val_ref[1, quarter].astype(F32)[own]
                val_re = jnp.concatenate([val_re] * bands, axis=0)
                val_im = jnp.concatenate([val_im] * bands, axis=0)
                re.append(val_re * con_re + val_im * con_im)
                im.append(val_re * con_im - val_im * con_re)
            a_re, a_im = re[0] + re[2], im[0] + im[2]
            b_re, b_im = re[0] - re[2], im[0] - im[2]
            c_re, c_im = re[1] + re[3], im[1] + im[3]
            d_re, d_im = re[1] - re[3], im[1] - im[3]
            made = [
                (a_re + c_re, a_im + c_im),
                (b_re + d_im, b_im - d_re),
                (a_re - c_re, a_im - c_im),
                (b_re - d_im, b_im + d_re),
            ]
            for residue in range(RADIX):
                for comp in range(2):
                    value = made[residue][comp]
                    high = value.astype(BF)
                    low = (value - high.astype(F32)).astype(BF)
                    at = comp * (half // 2) + band * block
                    x_ref[residue, at : at + block] = high
                    x_ref[residue, half + at : half + at + block] = low

    dot = functools.partial(jnp.dot, preferred_element_type=F32)
    x = x_ref[step]

    def accurate(which):
        main = dot(x, plane_ref[0, 0, which])
        return main[:half] + main[half:] + dot(x[:half], plane_ref[0, 1, which])

    cos_part = accurate(0)
    sin_part = accurate(1)
    quart = half // 2
    planes = jnp.concatenate(
        [cos_part[:quart] + sin_part[quart:], cos_part[quart:] - sin_part[:quart]], axis=0
    )
    high = planes.astype(BF)
    low = (planes - high.astype(F32)).astype(BF)
    total = dot(first_ref[0], high) + dot(first_ref[0], low) + dot(first_ref[1], high)
    out_ref[...] = total.astype(BF)


def pick_kernel(count, spec_ref, plane_at_ref, first_at_ref, weight_ref, plain_ref, scaled_ref):
    rows, depth = spec_ref.shape
    comps = rows // count
    place = plane_at_ref[0]
    width = place.shape[-1]
    total = jnp.zeros((rows, width), F32)
    chunk = 256 if depth % 256 == 0 else 128
    ident = lax.broadcasted_iota(jnp.int32, (chunk, width), 0)
    for start in range(0, depth, chunk):
        hot = jnp.where(ident == place - start, 1.0, 0.0).astype(BF)
        total += jnp.dot(spec_ref[:, start : start + chunk], hot, preferred_element_type=F32)
    freq = jnp.broadcast_to(first_at_ref[0], (comps, width))
    value = jnp.zeros((comps, width), F32)
    for k in range(count):
        value += jnp.where(freq == k, total[k * comps : (k + 1) * comps], 0.0)
    plain_ref[0] = value.astype(BF)
    scaled_ref[0] = (weight_ref[...] * value).astype(BF)


def outer_kernel(left_ref, right_ref, turned_ref, out_ref):
    left = left_ref[...]
    width = out_ref.shape[-1]
    out_ref[0] = jnp.dot(left, right_ref[...], preferred_element_type=F32)[:, :width]
    out_ref[1] = jnp.dot(left, turned_ref[...], preferred_element_type=F32)[:, :width]


def params(**kw):
    return pltpu.CompilerParams(vmem_limit_bytes=VMEM, **kw)


def largest(total, unit, most):
    return max(t for t in range(unit, most + 1, unit) if total % t == 0)


def on_device(valence, conduction, valence_slot_index, weights, sphere_index):
    rows = lax.axis_size("row")
    cols = lax.axis_size("col")
    nbands, nown = weights.shape
    pairs = nbands * nown
    count = NBOX
    square = count * count
    plane, first, part, wide = host_tables(count, pairs)

    def arrange(x):
        n = x.shape[0]
        x = x.reshape(n, 2, count, RADIX, part)
        return jnp.transpose(x, (1, 3, 0, 2, 4)).reshape(2, RADIX, n * count, part)

    stored = arrange(valence).reshape(2, RADIX, 1, count, part)
    me = lax.axis_index("row") * cols + lax.axis_index("col")
    mine = (valence_slot_index == me).reshape(1, 1, nbands, 1, 1)
    chosen = lax.psum(jnp.where(mine, stored, jnp.zeros_like(stored)), ("row", "col"))
    chosen = chosen.reshape(2, RADIX, nbands * count, part)
    states = arrange(conduction)

    size = 2 * pairs * count
    spectrum = pl.pallas_call(
        functools.partial(dft_kernel, nbands, count),
        grid=(RADIX,),
        in_specs=[
            pl.BlockSpec(chosen.shape, lambda r: (0, 0, 0, 0)),
            pl.BlockSpec(states.shape, lambda r: (0, 0, 0, 0)),
            pl.BlockSpec((1,) + plane.shape[1:], lambda r: (r, 0, 0, 0, 0)),
            pl.BlockSpec(first.shape, lambda r: (0, 0, 0)),
        ],
        out_specs=pl.BlockSpec((size, wide), lambda r: (0, r)),
        out_shape=jax.ShapeDtypeStruct((size, RADIX * wide), BF),
        scratch_shapes=[pltpu.VMEM((RADIX, 2 * size, part), BF)],
        compiler_params=params(),
    )(chosen, states, jnp.asarray(plane), jnp.asarray(first))

    ng = sphere_index.shape[0]
    unit = ng // cols
    unit_wide = -(-unit // 128) * 128
    tile = largest(unit_wide, 128, 256)
    freq_b = (sphere_index // count) % count
    place = (freq_b % RADIX) * wide + (freq_b // RADIX) * count + sphere_index % count
    pad = ((0, 0), (0, unit_wide - unit))
    place = jnp.pad(place.reshape(cols, unit), pad, constant_values=-1)[:, None]
    leading = jnp.pad((sphere_index // square).reshape(cols, unit), pad)[:, None]
    weight = jnp.tile(weights.reshape(pairs), 2)[:, None]
    shape = jax.ShapeDtypeStruct((cols, 2 * pairs, unit_wide), BF)
    index_spec = pl.BlockSpec((1, 1, tile), lambda u, t: (u, 0, t))
    value_spec = pl.BlockSpec((1, 2 * pairs, tile), lambda u, t: (u, 0, t))
    plain, scaled = pl.pallas_call(
        functools.partial(pick_kernel, count),
        grid=(cols, unit_wide // tile),
        in_specs=[
            pl.BlockSpec(spectrum.shape, lambda u, t: (0, 0)),
            index_spec,
            index_spec,
            pl.BlockSpec(weight.shape, lambda u, t: (0, 0)),
        ],
        out_specs=[value_spec, value_spec],
        out_shape=[shape, shape],
        compiler_params=params(),
    )(spectrum, place, leading, weight)

    per_row = cols // rows
    scaled = scaled.reshape(rows, per_row, 2 * pairs, unit_wide)
    regrouped = lax.all_to_all(scaled, "row", split_axis=0, concat_axis=0, tiled=True)
    row_block = lax.all_gather(regrouped, "col", axis=0)
    spread = lax.all_to_all(plain, "col", split_axis=0, concat_axis=0, tiled=True)
    right = lax.all_gather(spread, "row", axis=0)
    depth = rows * cols * 2 * pairs
    left = jnp.transpose(row_block[..., :unit], (2, 4, 1, 0, 3)).reshape(per_row * unit, depth)
    turned = jnp.concatenate([-right[:, :, pairs:], right[:, :, :pairs]], axis=2)
    right = right.reshape(depth, unit_wide)
    turned = turned.reshape(depth, unit_wide)
    nrows = per_row * unit
    high = largest(nrows, 16, 256)
    return pl.pallas_call(
        outer_kernel,
        grid=(nrows // high,),
        in_specs=[
            pl.BlockSpec((high, depth), lambda i: (i, 0)),
            pl.BlockSpec(right.shape, lambda i: (0, 0)),
            pl.BlockSpec(turned.shape, lambda i: (0, 0)),
        ],
        out_specs=pl.BlockSpec((2, high, unit), lambda i: (0, i, 0)),
        out_shape=jax.ShapeDtypeStruct((2, nrows, unit), F32),
        compiler_params=params(),
    )(left, right, turned)


def solution(mesh):
    placed = (
        P(("row", "col"), None, None),
        P(("row", "col"), None, None),
        P(),
        P(None, ("row", "col")),
        P(),
    )
    return jax.shard_map(
        on_device, mesh=mesh, in_specs=placed, out_specs=P(None, "row", "col"), check_vma=False
    )
```

time: 553 us -> 315 us (0.57); the launches traced: 545 us -> 314 us
  local copies, waits for them, and re-layouts: 224 us -> 20.6 us
  other arithmetic: 119 us -> 4.28 us
  waiting for transfers between devices: 73.6 us -> 168 us
  matrix products: 80.6 us -> 0 us
  Pallas kernels: 0 us -> 74.3 us
    gather x1 -> x0, local copies, waits for them, and re-layouts: 103 us -> none  [transform_pick(): picked = spectrum[first_freq, :, :, plane_freq]]
    psum x1, waiting for transfers between devices: 45.2 us -> 127 us  [on_device(): lax.psum(jnp.where(mine, stored, jnp.zeros_like(stored)), ('row', 'col'))]
    dot_general x5 -> x0, matrix products: 80.6 us -> none  [the longest x1 55.9 us: transform_pick(): jnp.dot(joined.reshape(pairs * count, 2 * square), plane_table(count), pr...]
    pallas_call x0 -> x3, Pallas kernels: none -> 74.3 us  [the longest x1 37.7 us: on_device(): pl.pallas_call(functools.partial(pick_kernel, count), grid=(cols, unit_wi...]
    dot_general x2 -> x0, local copies, waits for them, and re-layouts: 55.2 us -> none  [the longest x1 49.3 us: transform_pick(): jnp.einsum('kfad,pady->kfpy', axis_table(count), planes, precision=high)]
    neg x2 -> x1, other arithmetic: 47.8 us -> 1.37 us  [on_device(): -right[:, :, pairs:]]
    concatenate x2 -> x1, other arithmetic: 35.2 us -> 1.16 us  [on_device(): jnp.concatenate([-right[:, :, pairs:], right[:, :, :pairs]], axis=2)]
    unnamed x14 -> x6, local copies, waits for them, and re-layouts: 28.6 us -> 0.01 us
  transfers between devices with their start and end apart: 3 -> 3, of which waited for: 2 -> 3; matrix products, arithmetic and copies ran while one was open for 20% -> 3% of each run, Pallas kernels for 0% -> 0%
where the time goes in v1:
time: 315 us; the launch traced here: 314 us
  waiting for transfers between devices  168 us (53%)
  Pallas kernels  74.3 us (24%)
  blocking collectives  34.1 us (11%)
  local copies, waits for them, and re-layouts  20.6 us (7%)
  between operations  13.2 us (4%)
  other arithmetic  4.28 us (1%)
    psum x1, waiting for transfers between devices, on_device(): lax.psum(jnp.where(mine, stored, jnp.zeros_like(stored)), ('row', 'col'))  127 us
    pallas_call x1, Pallas kernels, on_device(): pl.pallas_call(functools.partial(pick_kernel, count), grid=(cols, unit_wi...  37.7 us
    all_gather x1, waiting for transfers between devices, on_device(): row_block = lax.all_gather(regrouped, 'col', axis=0)  27.1 us
    all_to_all x1, blocking collectives, on_device(): lax.all_to_all(scaled, 'row', split_axis=0, concat_axis=0, tiled=True)  22.4 us
    pallas_call x1, Pallas kernels, on_device(): pl.pallas_call(functools.partial(dft_kernel, nbands, count), grid=(RADIX,...  20.9 us
    pallas_call x1, Pallas kernels, on_device(): pl.pallas_call(outer_kernel, grid=(nrows // high,), in_specs=[pl.BlockSpe...  15.6 us
    all_gather x1, waiting for transfers between devices, on_device(): right = lax.all_gather(spread, 'row', axis=0)  13.6 us
    all_to_all x1, blocking collectives, on_device(): lax.all_to_all(plain, 'col', split_axis=0, concat_axis=0, tiled=True)  11.7 us
  transfers between devices with their start and end apart: 3, of which 3 were waited for; matrix products, arithmetic and copies ran while one was open for 3% of the time, Pallas kernels for 0%

profile of v1, /device:TPU:0, one launch (start us, length us, event | category | flops | bytes accessed | tf_op | source)
XLA Modules:
  0.0 314.4 jit_solution(6651358663519961690)
XLA Ops:
  6.5 0.0 copy-start.2
  6.5 0.0 copy-start.1
  6.5 0.0 copy-start
  6.5 0.0 all-reduce.4.cloned.1.call-start
  6.5 1.8 reshape.33
  8.3 0.1 copy.16
  8.4 0.7 broadcast_compare_fusion
  9.0 1.0 broadcast_select_fusion
  10.0 0.0 all-reduce.4.cloned.1.call-update
  10.0 0.0 all-gather.7.cloned.1.call-start
  10.1 0.0 copy-done.2
  10.1 0.1 tile.7
  10.2 0.7 broadcast_in_dim_tile.4.weight_ref
  10.8 0.0 copy-done.1
  10.8 0.1 add_select_fusion
  11.0 0.1 reshape.38
  11.1 0.6 broadcast_in_dim.38.first_at_ref
  11.7 0.1 reshape.37
  11.8 0.6 broadcast_in_dim.37.plane_at_ref
  12.5 0.0 copy-done
  12.5 3.0 reshape.35
  15.4 1.4 copy.17
  16.8 127.2 %all-reduce.4.cloned.1.call-done.val_ref = bf16[2,4,80,400]{3,2,1,0:T(8,128)(2,1)} async-done(((bf16[2,4,80,400]{3,2,1,0:T(8,128)(2,1)}), bf16[2,4,80,400]{3,2,1,0:T(8,128)(2,1)}) %all-reduce.4.cloned.1.call-update) | async-done | bytes 512016 | tf_op jit(solution)/shard_map/psum | solution.py:164
  144.0 20.9 %shard_map.73.spec_ref = bf16[640,2048]{1,0:T(8,128)(2,1)} custom-call(bf16[2,4,80,400]{3,2,1,0:T(8,128)(2,1)} %all-reduce.4.cloned.1.call-done.val_ref, bf16[2,4,160,400]{3,2,1,0:T(8,128)(2,1)} %bitcast.16, bf16[4,2,2,400,512]{4,3,2,1,0:T(8,128)(2,1)} %constant.70.clone.plane_ref, bf16[2,640,640]{2,1,0:T(8,128)(2,1)} %constant.71.clone.first_ref), custom_call_target="tpu_custom_call" | custom-call | tf_op jit(solution)/shard_map/pallas_call | solution.py:169
  164.9 37.7 %shard_map.74 = (bf16[8,16,1280]{2,1,0:T(8,128)(2,1)}, bf16[8,16,1280]{2,1,0:T(8,128)(2,1)}) custom-call(bf16[640,2048]{1,0:T(8,128)(2,1)} %shard_map.73.spec_ref, s32[8,1,1280]{2,1,0:T(1,128)} %broadcast_in_dim.37.plane_at_ref, s32[8,1,1280]{2,1,0:T(1,128)} %broadcast_in_dim.38.first_at_ref, f32[16,1]{1,0:T(8,128)} %broadcast_in_dim_tile.4.weight_ref), custom_call_target="tpu_custom_call" | custom-call | tf_op jit(solution)/shard_map/pallas_call | solution.py:197
  202.6 11.7 %all_to_all.10 = bf16[8,16,1280]{2,1,0:T(8,128)(2,1)} all-to-all(bf16[8,16,1280]{2,1,0:T(8,128)(2,1)} %get-tuple-element.8), channel_id=1, replica_groups=mesh['row'=4,'col'=8] {'col'}, dimensions={0} | all-to-all | bytes 655360 | tf_op jit(solution)/shard_map/all_to_all | solution.py:215
  214.3 0.0 all-gather.7.cloned.1.call-update
  214.3 0.0 all-gather.5.cloned.1.call-start
  214.4 22.4 %all_to_all.11 = bf16[4,2,16,1280]{3,2,1,0:T(8,128)(2,1)} all-to-all(bf16[4,2,16,1280]{3,2,1,0:T(8,128)(2,1)} %bitcast.23), channel_id=1, replica_groups=mesh['row'=4,'col'=8] {'row'}, dimensions={0} | all-to-all | bytes 655360 | tf_op jit(solution)/shard_map/all_to_all | solution.py:213
  236.7 0.0 all-gather.5.cloned.1.call-update
  236.8 13.6 %all-gather.7.cloned.1.call-done = bf16[32,16,1280]{2,1,0:T(8,128)(2,1)} async-done(((bf16[8,16,1280]{2,1,0:T(8,128)(2,1)}), bf16[32,16,1280]{2,1,0:T(8,128)(2,1)}) %all-gather.7.cloned.1.call-update) | async-done | bytes 1310736 | tf_op jit(solution)/shard_map/all_gather | solution.py:216
  250.4 1.4 slice_negate_fusion
  251.7 1.2 pad_maximum_fusion
  252.9 27.1 %all-gather.5.cloned.1.call-done = bf16[32,2,16,1280]{3,2,1,0:T(8,128)(2,1)} async-done(((bf16[4,2,16,1280]{3,2,1,0:T(8,128)(2,1)}), bf16[32,2,16,1280]{3,2,1,0:T(8,128)(2,1)}) %all-gather.5.cloned.1.call-update) | async-done | bytes 2621456 | tf_op jit(solution)/shard_map/all_gather | solution.py:214
  280.0 2.0 slice_bitcast_fusion
  282.0 2.6 copy.19
  284.6 3.1 reshape.40
  287.7 4.5 %copy.20.left_ref = bf16[2496,512]{1,0:T(8,128)(2,1)} copy(bf16[2496,512]{0,1:T(8,128)(2,1)} %reshape.40) | data formatting | bytes 5111808 | tf_op jit(solution)/shard_map/reshape | solution.py:218
  292.2 15.6 %shard_map.75 = f32[2,2496,1248]{2,1,0:T(8,128)} custom-call(bf16[2496,512]{1,0:T(8,128)(2,1)} %copy.20.left_ref, bf16[512,1280]{1,0:T(8,128)(2,1)} %bitcast.18, bf16[512,1280]{1,0:T(8,128)(2,1)} %bitcast.19), custom_call_target="tpu_custom_call" | custom-call | tf_op jit(solution)/shard_map/pallas_call | solution.py:224
  (3 shorter events, 0.0 us)
Async XLA Ops:
  6.5 3.5 %copy-start.2 = (f32[2,4]{1,0:T(2,128)S(1)}, f32[2,4]{1,0:T(2,128)}, u32[]{:S(2)}) copy-start(f32[2,4]{1,0:T(2,128)} %param.10) | copy-start | bytes 100
  6.5 4.3 %copy-start.1 = (s32[9984]{0:T(1024)S(1)}, s32[9984]{0:T(1024)}, u32[]{:S(2)}) copy-start(s32[9984]{0:T(1024)} %param.11) | copy-start | bytes 119812
  6.5 5.9 %copy-start = (bf16[4,2,64000]{2,1,0:T(2,128)(2,1)S(1)}, bf16[4,2,64000]{2,1,0:T(2,128)(2,1)}, u32[]{:S(2)}) copy-start(bf16[4,2,64000]{2,1,0:T(2,128)(2,1)} %param.8) | copy-start | bytes 3072004
  6.5 137.4 %all-reduce.4.cloned.1.call-start = ((), (), s32[]{:S(2)}) async-start(), calls=%async_computation.2 | async-start | bytes 1310720 | tf_op jit(solution)/shard_map/psum | solution.py:164
  10.0 240.3 %all-gather.7.cloned.1.call-start = ((), (), s32[]{:S(2)}) async-start(), calls=%async_computation.4 | async-start | bytes 1638400 | tf_op jit(solution)/shard_map/all_gather | solution.py:216
  214.3 65.6 %all-gather.5.cloned.1.call-start = ((), (), s32[]{:S(2)}) async-start(), calls=%async_computation.3 | async-start | bytes 2949120 | tf_op jit(solution)/shard_map/all_gather | solution.py:214
Sparse Core Ops, SparseCore 0:
  12.6 131.3 all-reduce.3
  214.4 35.8 all-gather.6
  252.4 27.5 all-gather.4

commit v2 on v1

--- a/solution.py
+++ b/solution.py
@@ -113,27 +113,46 @@
 def pick_kernel(count, spec_ref, plane_at_ref, first_at_ref, weight_ref, plain_ref, scaled_ref):
     rows, depth = spec_ref.shape
     comps = rows // count
-    place = plane_at_ref[0]
-    width = place.shape[-1]
-    total = jnp.zeros((rows, width), F32)
-    chunk = 256 if depth % 256 == 0 else 128
-    ident = lax.broadcasted_iota(jnp.int32, (chunk, width), 0)
-    for start in range(0, depth, chunk):
-        hot = jnp.where(ident == place - start, 1.0, 0.0).astype(BF)
-        total += jnp.dot(spec_ref[:, start : start + chunk], hot, preferred_element_type=F32)
-    freq = jnp.broadcast_to(first_at_ref[0], (comps, width))
-    value = jnp.zeros((comps, width), F32)
-    for k in range(count):
-        value += jnp.where(freq == k, total[k * comps : (k + 1) * comps], 0.0)
-    plain_ref[0] = value.astype(BF)
-    scaled_ref[0] = (weight_ref[...] * value).astype(BF)
-
-
-def outer_kernel(left_ref, right_ref, turned_ref, out_ref):
-    left = left_ref[...]
-    width = out_ref.shape[-1]
-    out_ref[0] = jnp.dot(left, right_ref[...], preferred_element_type=F32)[:, :width]
-    out_ref[1] = jnp.dot(left, turned_ref[...], preferred_element_type=F32)[:, :width]
+    width = plane_at_ref.shape[-1]
+    tile = largest(width, 128, 256)
+    ident = lax.broadcasted_iota(jnp.int32, (depth, tile), 0)
+    for start in range(0, width, tile):
+        at = slice(start, start + tile)
+        hot = jnp.where(ident == plane_at_ref[0, :, at], 1.0, 0.0).astype(BF)
+        total = jnp.dot(spec_ref[...], hot, preferred_element_type=F32)
+        freq = jnp.broadcast_to(first_at_ref[0, :, at], (comps, tile))
+        value = jnp.zeros((comps, tile), F32)
+        for k in range(count):
+            value += jnp.where(freq == k, total[k * comps : (k + 1) * comps], 0.0)
+        plain_ref[0, :, at] = value.astype(BF)
+        scaled_ref[0, :, at] = (weight_ref[...] * value).astype(BF)
+
+
+def outer_kernel(left_ref, right_ref, out_ref, left_at, right_at, turned_at):
+    rows, cols, comps, _ = right_ref.shape
+    high, width = out_ref.shape[1:]
+    step = pl.program_id(1)
+
+    @pl.when((pl.program_id(0) == 0) & (step == 0))
+    def _():
+        for col in range(cols):
+            for row in range(rows):
+                at = slice((col * rows + row) * comps, (col * rows + row + 1) * comps)
+                value = right_ref[row, col]
+                right_at[at] = value
+                wide = value.astype(F32)
+                half = comps // 2
+                turned = jnp.concatenate([-wide[half:], wide[:half]], axis=0)
+                turned_at[at] = turned.astype(BF)
+
+    @pl.when(step == 0)
+    def _():
+        left = left_ref[...]
+        left_at[...] = left.reshape(-1, left.shape[-1]).T
+
+    left = left_at[pl.ds(pl.multiple_of(step * high, 16), high)]
+    out_ref[0] = jnp.dot(left, right_at[...], preferred_element_type=F32)[:, :width]
+    out_ref[1] = jnp.dot(left, turned_at[...], preferred_element_type=F32)[:, :width]
 
 
 def params(**kw):
@@ -158,11 +177,13 @@
         x = x.reshape(n, 2, count, RADIX, part)
         return jnp.transpose(x, (1, 3, 0, 2, 4)).reshape(2, RADIX, n * count, part)
 
-    stored = arrange(valence).reshape(2, RADIX, 1, count, part)
     me = lax.axis_index("row") * cols + lax.axis_index("col")
-    mine = (valence_slot_index == me).reshape(1, 1, nbands, 1, 1)
-    chosen = lax.psum(jnp.where(mine, stored, jnp.zeros_like(stored)), ("row", "col"))
-    chosen = chosen.reshape(2, RADIX, nbands * count, part)
+    bands = []
+    for band in range(nbands):
+        mine = jnp.where(valence_slot_index[band] == me, valence[0], jnp.zeros_like(valence[0]))
+        bands.append(lax.psum(mine, ("row", "col")))
+    bands = lax.optimization_barrier(bands)
+    chosen = arrange(jnp.stack(bands))
     states = arrange(conduction)
 
     size = 2 * pairs * count
@@ -184,7 +205,6 @@
     ng = sphere_index.shape[0]
     unit = ng // cols
     unit_wide = -(-unit // 128) * 128
-    tile = largest(unit_wide, 128, 256)
     freq_b = (sphere_index // count) % count
     place = (freq_b % RADIX) * wide + (freq_b // RADIX) * count + sphere_index % count
     pad = ((0, 0), (0, unit_wide - unit))
@@ -192,16 +212,16 @@
     leading = jnp.pad((sphere_index // square).reshape(cols, unit), pad)[:, None]
     weight = jnp.tile(weights.reshape(pairs), 2)[:, None]
     shape = jax.ShapeDtypeStruct((cols, 2 * pairs, unit_wide), BF)
-    index_spec = pl.BlockSpec((1, 1, tile), lambda u, t: (u, 0, t))
-    value_spec = pl.BlockSpec((1, 2 * pairs, tile), lambda u, t: (u, 0, t))
+    index_spec = pl.BlockSpec((1, 1, unit_wide), lambda u: (u, 0, 0))
+    value_spec = pl.BlockSpec((1, 2 * pairs, unit_wide), lambda u: (u, 0, 0))
     plain, scaled = pl.pallas_call(
         functools.partial(pick_kernel, count),
-        grid=(cols, unit_wide // tile),
+        grid=(cols,),
         in_specs=[
-            pl.BlockSpec(spectrum.shape, lambda u, t: (0, 0)),
+            pl.BlockSpec(spectrum.shape, lambda u: (0, 0)),
             index_spec,
             index_spec,
-            pl.BlockSpec(weight.shape, lambda u, t: (0, 0)),
+            pl.BlockSpec(weight.shape, lambda u: (0, 0)),
         ],
         out_specs=[value_spec, value_spec],
         out_shape=[shape, shape],
@@ -215,24 +235,26 @@
     spread = lax.all_to_all(plain, "col", split_axis=0, concat_axis=0, tiled=True)
     right = lax.all_gather(spread, "row", axis=0)
     depth = rows * cols * 2 * pairs
-    left = jnp.transpose(row_block[..., :unit], (2, 4, 1, 0, 3)).reshape(per_row * unit, depth)
-    turned = jnp.concatenate([-right[:, :, pairs:], right[:, :, :pairs]], axis=2)
-    right = right.reshape(depth, unit_wide)
-    turned = turned.reshape(depth, unit_wide)
-    nrows = per_row * unit
-    high = largest(nrows, 16, 256)
+    high = largest(unit, 16, 256)
+    tiles = unit // high
     return pl.pallas_call(
         outer_kernel,
-        grid=(nrows // high,),
+        grid=(per_row, tiles),
         in_specs=[
-            pl.BlockSpec((high, depth), lambda i: (i, 0)),
-            pl.BlockSpec(right.shape, lambda i: (0, 0)),
-            pl.BlockSpec(turned.shape, lambda i: (0, 0)),
-        ],
-        out_specs=pl.BlockSpec((2, high, unit), lambda i: (0, i, 0)),
-        out_shape=jax.ShapeDtypeStruct((2, nrows, unit), F32),
+            pl.BlockSpec(
+                (cols, rows, None, 2 * pairs, unit_wide), lambda u, i: (0, 0, u, 0, 0)
+            ),
+            pl.BlockSpec(right.shape, lambda u, i: (0, 0, 0, 0)),
+        ],
+        out_specs=pl.BlockSpec((2, high, unit), lambda u, i: (0, u * tiles + i, 0)),
+        out_shape=jax.ShapeDtypeStruct((2, per_row * unit, unit), F32),
+        scratch_shapes=[
+            pltpu.VMEM((unit_wide, depth), BF),
+            pltpu.VMEM((depth, unit_wide), BF),
+            pltpu.VMEM((depth, unit_wide), BF),
+        ],
         compiler_params=params(),
-    )(left, right, turned)
+    )(row_block, right)
 
 
 def solution(mesh):

time: 315 us -> 302 us (0.959)
  local copies, waits for them, and re-layouts: 20.6 us -> 12 us
  Pallas kernels: 74.3 us -> 69.3 us
    reshape x2 -> x0, local copies, waits for them, and re-layouts: 7.62 us -> none  [on_device(): jnp.transpose(row_block[..., :unit], (2, 4, 1, 0, 3))]
    pallas_call x2, Pallas kernels: 53.3 us -> 48.3 us  [the longest x1 31.6 us: on_device(): pl.pallas_call(functools.partial(pick_kernel, count), grid=(cols,), in_sp...]
    transpose x2 -> x0, local copies, waits for them, and re-layouts: 4.62 us -> none  [on_device(): jnp.transpose(row_block[..., :unit], (2, 4, 1, 0, 3))]
    another operation x0 -> x4, local copies, waits for them, and re-layouts: none -> 3.44 us  [on_device(): chosen = arrange(jnp.stack(bands))]
    psum x1, waiting for transfers between devices: 127 us -> 124 us  [on_device(): bands.append(lax.psum(mine, ('row', 'col')))]
where the time goes in v2:
time: 302 us; the launch traced here: 301 us
  waiting for transfers between devices  167 us (55%)
  Pallas kernels  69.3 us (23%)
  blocking collectives  34.1 us (11%)
  between operations  14.4 us (5%)
  local copies, waits for them, and re-layouts  12 us (4%)
  other arithmetic  3.96 us (1%)
    psum x1, waiting for transfers between devices, on_device(): bands.append(lax.psum(mine, ('row', 'col')))  124 us
    pallas_call x1, Pallas kernels, on_device(): pl.pallas_call(functools.partial(pick_kernel, count), grid=(cols,), in_sp...  31.6 us
    all_gather x1, waiting for transfers between devices, on_device(): row_block = lax.all_gather(regrouped, 'col', axis=0)  29.6 us
    all_to_all x1, blocking collectives, on_device(): lax.all_to_all(scaled, 'row', split_axis=0, concat_axis=0, tiled=True)  22.4 us
    pallas_call x1, Pallas kernels, on_device(): pl.pallas_call(functools.partial(dft_kernel, nbands, count), grid=(RADIX,...  20.9 us
    pallas_call x1, Pallas kernels, on_device(): pl.pallas_call(outer_kernel, grid=(per_row, tiles), in_specs=[pl.BlockSpe...  16.8 us
    all_gather x1, waiting for transfers between devices, on_device(): right = lax.all_gather(spread, 'row', axis=0)  13.6 us
    all_to_all x1, blocking collectives, on_device(): lax.all_to_all(plain, 'col', split_axis=0, concat_axis=0, tiled=True)  11.7 us
  transfers between devices with their start and end apart: 3, of which 3 were waited for; matrix products, arithmetic and copies ran while one was open for 3% of the time, Pallas kernels for 0%

profile of v2, /device:TPU:0, one launch (start us, length us, event | category | flops | bytes accessed | tf_op | source)
XLA Modules:
  0.0 301.0 jit_solution(4603813461044709617)
XLA Ops:
  6.5 0.0 copy-start
  6.5 0.0 all-reduce.5.cloned.1.call-start
  6.5 1.3 fusion.12
  9.1 2.1 fusion.1
  11.2 0.0 all-reduce.5.cloned.1.call-update
  11.3 0.0 all-gather.7.cloned.1.call-start
  11.3 0.8 tile.7
  12.1 0.7 broadcast_in_dim_tile.4.weight_ref
  12.8 0.9 add_select_fusion
  13.7 0.1 reshape.34
  13.8 0.6 broadcast_in_dim.7.first_at_ref
  14.4 0.1 reshape.33
  14.5 0.6 broadcast_in_dim.6.plane_at_ref
  15.1 0.0 copy-done
  15.2 3.0 reshape.31
  18.1 1.3 copy.14
  19.5 124.0 %all-reduce.5.cloned.1.call-done = (bf16[2,64000]{1,0:T(2,128)(2,1)}, bf16[2,64000]{1,0:T(2,128)(2,1)}) async-done(((bf16[2,64000]{1,0:T(2,128)(2,1)}, bf16[2,64000]{1,0:T(2,128)(2,1)}), (bf16[2,64000]{1,0:T(2,128)(2,1)}, bf16[2,64000]{1,0:T(2,128)(2,1)})) %all-reduce.5.cloned.1.call-update) | async-done | bytes 512016 | tf_op jit(solution)/shard_map/psum | solution.py:184
  143.5 1.7 stack.9
  145.1 0.1 copy.12
  145.2 1.7 stack.10
  146.9 0.1 copy.13
  146.9 0.9 pad_maximum_fusion
  147.9 20.9 %shard_map.73.spec_ref = bf16[640,2048]{1,0:T(8,128)(2,1)} custom-call(bf16[2,4,80,400]{3,2,1,0:T(8,128)(2,1)} %bitcast.16, bf16[2,4,160,400]{3,2,1,0:T(8,128)(2,1)} %bitcast.15, bf16[4,2,2,400,512]{4,3,2,1,0:T(8,128)(2,1)} %constant.70.clone.plane_ref, bf16[2,640,640]{2,1,0:T(8,128)(2,1)} %constant.71.clone.first_ref), custom_call_target="tpu_custom_call" | custom-call | tf_op jit(solution)/shard_map/pallas_call | solution.py:190
  168.8 31.6 %shard_map.74 = (bf16[8,16,1280]{2,1,0:T(8,128)(2,1)}, bf16[8,16,1280]{2,1,0:T(8,128)(2,1)}) custom-call(bf16[640,2048]{1,0:T(8,128)(2,1)} %shard_map.73.spec_ref, s32[8,1,1280]{2,1,0:T(1,128)} %broadcast_in_dim.6.plane_at_ref, s32[8,1,1280]{2,1,0:T(1,128)} %broadcast_in_dim.7.first_at_ref, f32[16,1]{1,0:T(8,128)} %broadcast_in_dim_tile.4.weight_ref), custom_call_target="tpu_custom_call" | custom-call | tf_op jit(solution)/shard_map/pallas_call | solution.py:217
  200.4 11.7 %all_to_all.10 = bf16[8,16,1280]{2,1,0:T(8,128)(2,1)} all-to-all(bf16[8,16,1280]{2,1,0:T(8,128)(2,1)} %get-tuple-element.12), channel_id=1, replica_groups=mesh['row'=4,'col'=8] {'col'}, dimensions={0} | all-to-all | bytes 655360 | tf_op jit(solution)/shard_map/all_to_all | solution.py:235
  212.0 0.0 all-gather.7.cloned.1.call-update
  212.1 0.0 all-gather.5.cloned.1.call-start
  212.1 22.4 %all_to_all.11 = bf16[4,2,16,1280]{3,2,1,0:T(8,128)(2,1)} all-to-all(bf16[4,2,16,1280]{3,2,1,0:T(8,128)(2,1)} %bitcast.19), channel_id=1, replica_groups=mesh['row'=4,'col'=8] {'row'}, dimensions={0} | all-to-all | bytes 655360 | tf_op jit(solution)/shard_map/all_to_all | solution.py:233
  234.5 0.0 all-gather.5.cloned.1.call-update
  234.5 13.6 %all-gather.7.cloned.1.call-done = bf16[32,16,1280]{2,1,0:T(8,128)(2,1)} async-done(((bf16[8,16,1280]{2,1,0:T(8,128)(2,1)}), bf16[32,16,1280]{2,1,0:T(8,128)(2,1)}) %all-gather.7.cloned.1.call-update) | async-done | bytes 1310736 | tf_op jit(solution)/shard_map/all_gather | solution.py:236
  248.1 29.6 %all-gather.5.cloned.1.call-done = bf16[32,2,16,1280]{3,2,1,0:T(8,128)(2,1)} async-done(((bf16[4,2,16,1280]{3,2,1,0:T(8,128)(2,1)}), bf16[32,2,16,1280]{3,2,1,0:T(8,128)(2,1)}) %all-gather.5.cloned.1.call-update) | async-done | bytes 2621456 | tf_op jit(solution)/shard_map/all_gather | solution.py:234
  277.7 16.8 %shard_map.75 = f32[2,2496,1248]{2,1,0:T(8,128)} custom-call(bf16[8,4,2,16,1280]{4,3,2,1,0:T(8,128)(2,1)} %bitcast.17, bf16[4,8,16,1280]{3,2,1,0:T(8,128)(2,1)} %bitcast.18), custom_call_target="tpu_custom_call" | custom-call | tf_op jit(solution)/shard_map/pallas_call | solution.py:240
  (3 shorter events, 0.0 us)
Async XLA Ops:
  6.5 8.6 %copy-start = (bf16[4,2,64000]{2,1,0:T(2,128)(2,1)S(1)}, bf16[4,2,64000]{2,1,0:T(2,128)(2,1)}, u32[]{:S(2)}) copy-start(bf16[4,2,64000]{2,1,0:T(2,128)(2,1)} %param.8) | copy-start | bytes 3072004
  6.5 136.9 %all-reduce.5.cloned.1.call-start = ((), (), s32[]{:S(2)}) async-start(), calls=%async_computation.4 | async-start | bytes 1024000 | tf_op jit(solution)/shard_map/psum | solution.py:184
  11.3 236.9 %all-gather.7.cloned.1.call-start = ((), (), s32[]{:S(2)}) async-start(), calls=%async_computation.3 | async-start | bytes 1638400 | tf_op jit(solution)/shard_map/all_gather | solution.py:236
  212.1 65.6 %all-gather.5.cloned.1.call-start = ((), (), s32[]{:S(2)}) async-start(), calls=%async_computation.2 | async-start | bytes 2949120 | tf_op jit(solution)/shard_map/all_gather | solution.py:234
Sparse Core Ops, SparseCore 0:
  12.7 130.7 all-reduce.4
  212.2 35.8 all-gather.6
  250.2 27.4 all-gather.4

commit v3 on v2

--- a/solution.py
+++ b/solution.py
@@ -128,7 +128,7 @@
         scaled_ref[0, :, at] = (weight_ref[...] * value).astype(BF)
 
 
-def outer_kernel(left_ref, right_ref, out_ref, left_at, right_at, turned_at):
+def outer_kernel(here_ref, left_ref, right_ref, out_ref, left_at, right_at, turned_at):
     rows, cols, comps, _ = right_ref.shape
     high, width = out_ref.shape[1:]
     step = pl.program_id(1)
@@ -138,7 +138,7 @@
         for col in range(cols):
             for row in range(rows):
                 at = slice((col * rows + row) * comps, (col * rows + row + 1) * comps)
-                value = right_ref[row, col]
+                value = right_ref[lax.rem(here_ref[0] + rows - row, rows), col]
                 right_at[at] = value
                 wide = value.astype(F32)
                 half = comps // 2
@@ -178,12 +178,19 @@
         return jnp.transpose(x, (1, 3, 0, 2, 4)).reshape(2, RADIX, n * count, part)
 
     me = lax.axis_index("row") * cols + lax.axis_index("col")
-    bands = []
-    for band in range(nbands):
-        mine = jnp.where(valence_slot_index[band] == me, valence[0], jnp.zeros_like(valence[0]))
-        bands.append(lax.psum(mine, ("row", "col")))
+    points = valence.shape[-1]
+    lines = nbands * 2 * points // 128
+    share = -(-lines // (cols * 16)) * 16
+    stored = valence.reshape(1, 2, points // 128, 128)
+    mine = (valence_slot_index == me).reshape(nbands, 1, 1, 1)
+    blocks = jnp.where(mine, stored, jnp.zeros_like(stored)).reshape(lines, 128)
+    blocks = jnp.pad(blocks, ((0, cols * share - lines), (0, 0))).reshape(cols, share, 128)
+    blocks = lax.all_to_all(blocks, "col", split_axis=0, concat_axis=0, tiled=True)
+    block = jnp.sum(blocks, axis=0, dtype=F32).astype(BF)
+    block = jnp.sum(lax.all_gather(block, "row", axis=0), axis=0, dtype=F32).astype(BF)
+    bands = lax.all_gather(block, "col", axis=0, tiled=True)
     bands = lax.optimization_barrier(bands)
-    chosen = arrange(jnp.stack(bands))
+    chosen = arrange(bands[:lines].reshape(nbands, 2, points))
     states = arrange(conduction)
 
     size = 2 * pairs * count
@@ -230,7 +237,15 @@
 
     per_row = cols // rows
     scaled = scaled.reshape(rows, per_row, 2 * pairs, unit_wide)
-    regrouped = lax.all_to_all(scaled, "row", split_axis=0, concat_axis=0, tiled=True)
+    here = lax.axis_index("row")
+    parts = []
+    for shift in range(rows):
+        part_out = lax.dynamic_index_in_dim(scaled, (here + shift) % rows, 0, keepdims=False)
+        if shift > 0:
+            hops = [(row, (row + shift) % rows) for row in range(rows)]
+            part_out = lax.ppermute(part_out, "row", hops)
+        parts.append(part_out)
+    regrouped = jnp.stack(parts)
     row_block = lax.all_gather(regrouped, "col", axis=0)
     spread = lax.all_to_all(plain, "col", split_axis=0, concat_axis=0, tiled=True)
     right = lax.all_gather(spread, "row", axis=0)
@@ -241,6 +256,7 @@
         outer_kernel,
         grid=(per_row, tiles),
         in_specs=[
+            pl.BlockSpec(memory_space=pltpu.SMEM),
             pl.BlockSpec(
                 (cols, rows, None, 2 * pairs, unit_wide), lambda u, i: (0, 0, u, 0, 0)
             ),
@@ -254,7 +270,7 @@
             pltpu.VMEM((depth, unit_wide), BF),
         ],
         compiler_params=params(),
-    )(row_block, right)
+    )(here.astype(jnp.int32).reshape(1), row_block, right)
 
 
 def solution(mesh):

time: 302 us -> 203 us (0.67)
  waiting for transfers between devices: 167 us -> 61.3 us
  starting transfers between devices: 0.09 us -> 9.7 us
    psum x1 -> x0, waiting for transfers between devices: 124 us -> none  [on_device(): bands.append(lax.psum(mine, ('row', 'col')))]
    all_gather x0 -> x2, blocking collectives: none -> 23.2 us  [the longest x1 14.7 us: on_device(): lax.all_gather(block, 'row', axis=0)]
    all_to_all x1 -> x0, blocking collectives: 22.4 us -> none  [on_device(): lax.all_to_all(scaled, 'row', split_axis=0, concat_axis=0, tiled=True)]
    ppermute x0 -> x3, waiting for transfers between devices: none -> 10.9 us  [on_device(): part_out = lax.ppermute(part_out, 'row', hops)]
    all_to_all x0 -> x1, starting transfers between devices: none -> 5.17 us  [on_device(): lax.all_to_all(blocks, 'col', split_axis=0, concat_axis=0, tiled=True)]
    ppermute x0 -> x3, starting transfers between devices: none -> 4.45 us  [on_device(): part_out = lax.ppermute(part_out, 'row', hops)]
  transfers between devices with their start and end apart: 3 -> 6, of which waited for: 3 -> 5; matrix products, arithmetic and copies ran while one was open for 3% -> 4% of each run, Pallas kernels for 0% -> 0%
where the time goes in v3:
time: 203 us
  Pallas kernels  69.3 us (34%)
  waiting for transfers between devices  61.3 us (30%)
  blocking collectives  34.8 us (17%)
  between operations  13.6 us (7%)
  local copies, waits for them, and re-layouts  12.3 us (6%)
  starting transfers between devices  9.7 us (5%)
    pallas_call x1, Pallas kernels, on_device(): pl.pallas_call(functools.partial(pick_kernel, count), grid=(cols,), in_sp...  31.6 us
    all_gather x1, waiting for transfers between devices, on_device(): row_block = lax.all_gather(regrouped, 'col', axis=0)  30.8 us
    pallas_call x1, Pallas kernels, on_device(): pl.pallas_call(functools.partial(dft_kernel, nbands, count), grid=(RADIX,...  20.9 us
    pallas_call x1, Pallas kernels, on_device(): pl.pallas_call(outer_kernel, grid=(per_row, tiles), in_specs=[pl.BlockSpe...  16.8 us
    all_gather x1, waiting for transfers between devices, on_device(): right = lax.all_gather(spread, 'row', axis=0)  16.6 us
    all_gather x1, blocking collectives, on_device(): lax.all_gather(block, 'row', axis=0)  14.7 us
    all_to_all x1, blocking collectives, on_device(): lax.all_to_all(plain, 'col', split_axis=0, concat_axis=0, tiled=True)  11.7 us
    ppermute x3, waiting for transfers between devices, on_device(): part_out = lax.ppermute(part_out, 'row', hops)  10.9 us
  transfers between devices with their start and end apart: 6, of which 5 were waited for; matrix products, arithmetic and copies ran while one was open for 4% of the time, Pallas kernels for 0%

profile of v3, /device:TPU:0, one launch (start us, length us, event | category | flops | bytes accessed | tf_op | source)
XLA Modules:
  0.0 203.0 jit_solution(9909995014822446575)
XLA Ops:
  6.5 0.7 broadcast_compare_fusion
  7.2 0.1 broadcast_in_dim.39
  7.3 0.1 broadcast_in_dim.40
  7.4 0.0 copy-start.2
  7.4 0.0 copy-start.1
  7.4 1.1 broadcast_in_dim.42
  8.5 0.0 copy-start
  8.5 0.1 broadcast_in_dim.43
  8.6 0.1 broadcast_in_dim.44
  8.7 0.3 broadcast_select_fusion
  9.0 0.8 pad.11
  9.9 5.2 %all-to-all-start = ((bf16[8,256,128]{2,1,0:T(8,128)(2,1)}), bf16[8,256,128]{2,1,0:T(8,128)(2,1)S(1)}, u32[]{:S(2)}, u32[]{:S(2)}) async-start(bf16[8,256,128]{2,1,0:T(8,128)(2,1)} %bitcast.1), calls=%async_computation | async-start | bytes 1048576 | tf_op jit(solution)/shard_map/all_to_all | solution.py:188
  15.0 0.0 all-gather.8.cloned.1.call-start
  15.1 0.0 copy-done.2
  15.1 0.1 tile.7
  15.2 0.7 broadcast_in_dim_tile.4.weight_ref
  15.9 0.0 copy-done.1
  15.9 0.1 add_select_fusion
  16.0 0.1 reshape.39
  16.1 0.6 broadcast_in_dim.47.first_at_ref
  16.7 0.1 reshape.38
  16.9 0.6 broadcast_in_dim.46.plane_at_ref
  17.5 0.0 copy-done
  17.5 3.0 %reshape.36 = bf16[4,2,40,4,400]{4,3,2,1,0:T(4,128)(2,1)S(1)} reshape(bf16[4,2,64000]{2,1,0:T(2,128)(2,1)S(1)} %copy-done) | data formatting | bytes 2048000 | tf_op jit(solution)/shard_map/reshape | solution.py:177
  20.5 1.4 copy.17
  21.8 3.0 %all-to-all-done = bf16[8,256,128]{2,1,0:T(8,128)(2,1)S(1)} async-done(((bf16[8,256,128]{2,1,0:T(8,128)(2,1)}), bf16[8,256,128]{2,1,0:T(8,128)(2,1)S(1)}, u32[]{:S(2)}, u32[]{:S(2)}) %all-to-all-start) | async-done | bytes 524320 | tf_op jit(solution)/shard_map/all_to_all | solution.py:188
  24.8 0.1 reduce_sum.24
  24.9 14.7 %all-gather = bf16[1024,128]{1,0:T(8,128)(2,1)S(1)} all-gather(bf16[256,128]{1,0:T(8,128)(2,1)S(1)} %reduce_sum.24), channel_id=2, replica_groups=mesh['row'=4,'col'=8] {'row'}, dimensions={0}, use_global_device_ids=true | all-gather | bytes 327680 | tf_op jit(solution)/shard_map/all_gather | solution.py:190
  39.6 8.5 %all_gather.23 = bf16[2048,128]{1,0:T(8,128)(2,1)S(1)} all-gather(bf16[256,128]{1,0:T(8,128)(2,1)S(1)} %reduce_sum.25), channel_id=1, replica_groups=mesh['row'=4,'col'=8] {'col'}, dimensions={0}, use_global_device_ids=true | all-gather | bytes 589824 | tf_op jit(solution)/shard_map/all_gather | solution.py:191
  48.1 1.3 reshape_reshape.3
  49.5 1.0 copy.16
  50.4 20.9 %shard_map.73.spec_ref = bf16[640,2048]{1,0:T(8,128)(2,1)} custom-call(bf16[2,4,80,400]{3,2,1,0:T(8,128)(2,1)} %bitcast.21, bf16[2,4,160,400]{3,2,1,0:T(8,128)(2,1)} %bitcast.20, bf16[4,2,2,400,512]{4,3,2,1,0:T(8,128)(2,1)} %constant.105.clone.plane_ref, bf16[2,640,640]{2,1,0:T(8,128)(2,1)} %constant.106.clone.first_ref), custom_call_target="tpu_custom_call" | custom-call | tf_op jit(solution)/shard_map/pallas_call | solution.py:197
  71.3 31.6 %shard_map.74 = (bf16[8,16,1280]{2,1,0:T(8,128)(2,1)}, bf16[8,16,1280]{2,1,0:T(8,128)(2,1)}) custom-call(bf16[640,2048]{1,0:T(8,128)(2,1)} %shard_map.73.spec_ref, s32[8,1,1280]{2,1,0:T(1,128)} %broadcast_in_dim.46.plane_at_ref, s32[8,1,1280]{2,1,0:T(1,128)} %broadcast_in_dim.47.first_at_ref, f32[16,1]{1,0:T(8,128)} %broadcast_in_dim_tile.4.weight_ref), custom_call_target="tpu_custom_call" | custom-call | tf_op jit(solution)/shard_map/pallas_call | solution.py:224
  102.9 11.7 %all_to_all.10 = bf16[8,16,1280]{2,1,0:T(8,128)(2,1)} all-to-all(bf16[8,16,1280]{2,1,0:T(8,128)(2,1)} %get-tuple-element.8), channel_id=1, replica_groups=mesh['row'=4,'col'=8] {'col'}, dimensions={0} | all-to-all | bytes 655360 | tf_op jit(solution)/shard_map/all_to_all | solution.py:250
  114.6 0.0 all-gather.8.cloned.1.call-update
  114.6 0.0 all-gather.6.cloned.1.call-start
  114.7 1.0 constant_dynamic-slice_fusion
  115.8 3.8 %collective-permute-start.2 = (bf16[2,16,1280]{2,1,0:T(8,128)(2,1)S(1)}, bf16[2,16,1280]{2,1,0:T(8,128)(2,1)S(1)}, u32[]{:S(2)}, u32[]{:S(2)}) collective-permute-start(bf16[2,16,1280]{2,1,0:T(8,128)(2,1)S(1)} %get-tuple-element.10), channel_id=1, source_target_pairs={{0,24},{8,0},{16,8},{24,16},{1,25},{9,1},{17,9},{25,17},{2,26},{10... | collective-permute-start | bytes 245768 | tf_op jit(solution)/shard_map/ppermute | solution.py:246
  119.6 0.0 collective-permute-start.1
  119.6 0.6 collective-permute-start
  120.2 2.3 %collective-permute-done.2 = bf16[2,16,1280]{2,1,0:T(8,128)(2,1)S(1)} collective-permute-done((bf16[2,16,1280]{2,1,0:T(8,128)(2,1)S(1)}, bf16[2,16,1280]{2,1,0:T(8,128)(2,1)S(1)}, u32[]{:S(2)}, u32[]{:S(2)}) %collective-permute-start.2) | collective-permute-done | bytes 81952 | tf_op jit(solution)/shard_map/ppermute | solution.py:246
  122.5 8.6 %collective-permute-done.1 = bf16[2,16,1280]{2,1,0:T(8,128)(2,1)S(1)} collective-permute-done((bf16[2,16,1280]{2,1,0:T(8,128)(2,1)S(1)}, bf16[2,16,1280]{2,1,0:T(8,128)(2,1)S(1)}, u32[]{:S(2)}, u32[]{:S(2)}) %collective-permute-start.1) | collective-permute-done | bytes 81952 | tf_op jit(solution)/shard_map/ppermute | solution.py:246
  131.1 0.0 collective-permute-done
  131.2 0.8 pad_maximum_fusion
  131.9 0.0 all-gather.6.cloned.1.call-update
  131.9 16.6 %all-gather.8.cloned.1.call-done = bf16[32,16,1280]{2,1,0:T(8,128)(2,1)} async-done(((bf16[8,16,1280]{2,1,0:T(8,128)(2,1)}), bf16[32,16,1280]{2,1,0:T(8,128)(2,1)}) %all-gather.8.cloned.1.call-update) | async-done | bytes 1310736 | tf_op jit(solution)/shard_map/all_gather | solution.py:251
  148.6 30.8 %all-gather.6.cloned.1.call-done = bf16[32,2,16,1280]{3,2,1,0:T(8,128)(2,1)} async-done(((bf16[4,2,16,1280]{3,2,1,0:T(8,128)(2,1)}), bf16[32,2,16,1280]{3,2,1,0:T(8,128)(2,1)}) %all-gather.6.cloned.1.call-update) | async-done | bytes 2621456 | tf_op jit(solution)/shard_map/all_gather | solution.py:249
  179.4 16.8 %shard_map.75 = f32[2,2496,1248]{2,1,0:T(8,128)} custom-call(s32[1]{0:T(128)} %bitcast.here_ref, bf16[8,4,2,16,1280]{4,3,2,1,0:T(8,128)(2,1)} %bitcast.23, bf16[4,8,16,1280]{3,2,1,0:T(8,128)(2,1)} %bitcast.24), custom_call_target="tpu_custom_call" | custom-call | tf_op jit(solution)/shard_map/pallas_call | solution.py:255
  (5 shorter events, 0.1 us)
Async XLA Ops:
  7.4 7.7 %copy-start.2 = (f32[2,4]{1,0:T(2,128)S(1)}, f32[2,4]{1,0:T(2,128)}, u32[]{:S(2)}) copy-start(f32[2,4]{1,0:T(2,128)} %param.10) | copy-start | bytes 100
  7.4 8.5 %copy-start.1 = (s32[9984]{0:T(1024)S(1)}, s32[9984]{0:T(1024)}, u32[]{:S(2)}) copy-start(s32[9984]{0:T(1024)} %param.11) | copy-start | bytes 119812
  8.5 9.0 %copy-start = (bf16[4,2,64000]{2,1,0:T(2,128)(2,1)S(1)}, bf16[4,2,64000]{2,1,0:T(2,128)(2,1)}, u32[]{:S(2)}) copy-start(bf16[4,2,64000]{2,1,0:T(2,128)(2,1)} %param.8) | copy-start | bytes 3072004
  9.9 14.9 %all-to-all-start = ((bf16[8,256,128]{2,1,0:T(8,128)(2,1)}), bf16[8,256,128]{2,1,0:T(8,128)(2,1)S(1)}, u32[]{:S(2)}, u32[]{:S(2)}) async-start(bf16[8,256,128]{2,1,0:T(8,128)(2,1)} %bitcast.1), calls=%async_computation | async-start | bytes 1048576 | tf_op jit(solution)/shard_map/all_to_all | solution.py:188
  15.0 133.5 %all-gather.8.cloned.1.call-start = ((), (), s32[]{:S(2)}) async-start(), calls=%async_computation.3 | async-start | bytes 1638400 | tf_op jit(solution)/shard_map/all_gather | solution.py:251
  114.6 64.7 %all-gather.6.cloned.1.call-start = ((), (), s32[]{:S(2)}) async-start(), calls=%async_computation.2 | async-start | bytes 2949120 | tf_op jit(solution)/shard_map/all_gather | solution.py:249
  115.8 6.7 %collective-permute-start.2 = (bf16[2,16,1280]{2,1,0:T(8,128)(2,1)S(1)}, bf16[2,16,1280]{2,1,0:T(8,128)(2,1)S(1)}, u32[]{:S(2)}, u32[]{:S(2)}) collective-permute-start(bf16[2,16,1280]{2,1,0:T(8,128)(2,1)S(1)} %get-tuple-element.10), channel_id=1, source_target_pairs={{0,24},{8,0},{16,8},{24,16},{1,25},{9,1},{17,9},{25,17},{2,26},{10... | collective-permute-start | bytes 245768 | tf_op jit(solution)/shard_map/ppermute | solution.py:246
  119.6 11.6 %collective-permute-start.1 = (bf16[2,16,1280]{2,1,0:T(8,128)(2,1)S(1)}, bf16[2,16,1280]{2,1,0:T(8,128)(2,1)S(1)}, u32[]{:S(2)}, u32[]{:S(2)}) collective-permute-start(bf16[2,16,1280]{2,1,0:T(8,128)(2,1)S(1)} %get-tuple-element.11), channel_id=1, source_target_pairs={{0,16},{8,24},{16,0},{24,8},{1,17},{9,25},{17,1},{25,9},{2,18},{10... | collective-permute-start | bytes 245768 | tf_op jit(solution)/shard_map/ppermute | solution.py:246
  119.6 11.6 %collective-permute-start = (bf16[2,16,1280]{2,1,0:T(8,128)(2,1)S(1)}, bf16[2,16,1280]{2,1,0:T(8,128)(2,1)S(1)}, u32[]{:S(2)}, u32[]{:S(2)}) collective-permute-start(bf16[2,16,1280]{2,1,0:T(8,128)(2,1)S(1)} %get-tuple-element.12), channel_id=1, source_target_pairs={{0,8},{8,16},{16,24},{24,0},{1,9},{9,17},{17,25},{25,1},{2,10},{10... | collective-permute-start | bytes 245768 | tf_op jit(solution)/shard_map/ppermute | solution.py:246
Sparse Core Ops, SparseCore 0:
  114.8 33.7 all-gather.7
  150.4 28.8 all-gather.5
